TPU v7x, 32 devices: a whole 2x2x4 slice. The times are simulated.
32 devices in a mesh: blk: 8 (over z, y), par: 4 (over x, core).
Axes of the slice: x: 2, y: 2, z: 4, core: 2. Of those that a mesh axis runs over, the one named last changes fastest.
Arguments:
- log_derivs: float32 [2048, 4096], P('blk', 'par'), may hold values from -0.09375 to 0.09375
- energies: float32 [2048], P('blk'), may hold values from -6 to 6
Outputs:
- panel_tiles: float32 [2048, 256], P('blk')
- energies_next: float32 [2048], P('blk')
- diagonal_next: float32 [2048, 256], P(('blk', 'par'))
- neighbour_next: float32 [2048, 256], P(('blk', 'par'))
All inputs are finite; a program needn't handle non-finite values.
Results may differ from a plain program's by a relative error of at most 0.00011.
Values sent between devices are 32-bit elements; how exact they have to be, the bound alone decides.
A program may use at most 64 MiB of HBM per device.

v0:
```python
import jax
import jax.numpy as jnp
from jax import lax
from jax.sharding import PartitionSpec as P

ridge_shift = 0.05


def from_root(value, axis, source):
    kept = jnp.where(lax.axis_index(axis) == source, value, 0).astype(value.dtype)
    return lax.psum(kept, axis)


def passed_along(block, axis, distance):
    devices = range(lax.axis_size(axis))
    route = [((i - distance) % len(devices), i) for i in devices]
    return lax.ppermute(block, axis, route)


def kernel_tile(left_rows, right_rows):
    return jnp.dot(
        left_rows, right_rows.T, precision=lax.Precision.HIGHEST, preferred_element_type=jnp.float32
    )


def panel_solve(pivot_factor, cross_tile):
    return lax.linalg.triangular_solve(
        pivot_factor, cross_tile, left_side=False, lower=True, transpose_a=True
    )


def on_device(log_derivs, energies):
    block_size = log_derivs.shape[0]
    share_rows = block_size // lax.axis_size("par")
    row_start = lax.axis_index("par") * share_rows
    lead_rows = from_root(log_derivs, "blk", 0)
    lead_energy = from_root(energies, "blk", 0)
    prev_rows = passed_along(log_derivs, "blk", 1)
    cross_part = kernel_tile(log_derivs, lead_rows)
    self_part = kernel_tile(log_derivs, log_derivs)
    cycle_part = kernel_tile(log_derivs, prev_rows)
    pivot_part = kernel_tile(lead_rows, lead_rows)
    unit_full = jnp.eye(block_size, dtype=jnp.float32)
    cross_sum, self_sum, cycle_sum, pivot_sum = lax.psum(
        (cross_part, self_part, cycle_part, pivot_part), "par"
    )
    pivot_factor = jnp.linalg.cholesky(pivot_sum + ridge_shift * unit_full)
    panel_full = panel_solve(pivot_factor, cross_sum)
    panel_part = lax.dynamic_slice_in_dim(panel_full, row_start, share_rows, 0)
    self_rows = lax.dynamic_slice_in_dim(self_sum, row_start, share_rows, 0)
    cycle_rows = lax.dynamic_slice_in_dim(cycle_sum, row_start, share_rows, 0)
    back_sum = lax.psum(kernel_tile(prev_rows, lead_rows), "par")
    panel_prev = panel_solve(pivot_factor, back_sum)
    unit_rows = (
        lax.broadcasted_iota(jnp.int32, (share_rows, block_size), 0) + row_start
        == lax.broadcasted_iota(jnp.int32, (share_rows, block_size), 1)
    ).astype(jnp.float32)
    diagonal_next = self_rows + ridge_shift * unit_rows - kernel_tile(panel_part, panel_full)
    neighbour_next = cycle_rows - kernel_tile(panel_part, panel_prev)
    lead_solve = lax.linalg.triangular_solve(
        pivot_factor, lead_energy[:, None], left_side=True, lower=True
    )[:, 0]
    remainder = energies - jnp.dot(
        panel_full, lead_solve, precision=lax.Precision.HIGHEST, preferred_element_type=jnp.float32
    )
    energies_next = jnp.where(lax.axis_index("blk") == 0, lead_solve, remainder)
    return (panel_full, energies_next, diagonal_next, neighbour_next)


def solution(mesh):
    placed = (P("blk", "par"), P("blk"))
    return jax.shard_map(
        on_device,
        mesh=mesh,
        in_specs=placed,
        out_specs=(P("blk", None), P("blk"), P(("blk", "par"), None), P(("blk", "par"), None)),
        check_vma=False,
    )
```

profile of v0, /device:TPU:27, one launch (start us, length us, event | category | flops | bytes accessed | tf_op | source)
XLA Modules:
  0.0 230.8 jit_solution(15796298928775317836)
XLA Ops:
  7.2 1.2 broadcast_select_fusion
  8.4 1.1 copy-done
  9.6 1.2 collective-permute-start
  10.8 1.8 fusion.36
  12.6 90.7 %all-reduce.5.cloned.1.call-done = f32[256,1024]{1,0:T(8,128)} async-done(((f32[256,1024]{1,0:T(8,128)}), f32[256,1024]{1,0:T(8,128)}) %all-reduce.5.cloned.1.call-update) | async-done | bytes 1048592 | tf_op jit(solution)/shard_map/psum | solution.py:11
  103.3 3.0 %convolution_bitcast_fusion.1 = f32[256,256]{0,1:T(8,128)} fusion(f32[256,1024]{1,0:T(8,128)} %all-reduce.5.cloned.1.call-done, f32[256,1024]{1,0:T(8,128)S(1)} %copy-done), kind=kOutput, calls=%fused_computation.3 | convolution fusion | flops 805306368 | bytes 2359296 | tf_op jit(solution)/shard_map/dot_general | solution.py:21
  106.3 1.7 fusion.35
  108.1 1.7 convolution_bitcast_fusion
  109.8 1.7 fusion.37
  111.6 0.7 copy-done.5
  112.3 13.9 %psum.52 = f32[256]{0:T(256)S(1)} all-reduce(f32[256]{0:T(256)S(1)} %broadcast_select_fusion.1), channel_id=1, replica_groups=mesh['blk'=8,'par'=4] {'blk'}, use_global_device_ids=true, to_apply=%region_7.9 | all-reduce | flops 256 | bytes 2048 | tf_op jit(solution)/shard_map/psum | solution.py:11
  126.2 26.5 %all-reduce.7.cloned.1.call-done = (f32[256,256]{0,1:T(8,128)}, f32[256,256]{0,1:T(8,128)}, f32[256,256]{1,0:T(8,128)}, f32[256,256]{1,0:T(8,128)}, f32[256,256]{0,1:T(8,128)}) async-done(((f32[256,256]{0,1:T(8,128)}, f32[256,256]{0,1:T(8,128)}, f32[256,256]{1,0:T(8,128)}, f32[256,256]{1,0:T(8,128)}, f32[256,256]{0,1:T(8,128)}), (f32[256,256]{0,1:T(8,128)}, f32[256,256]{0,1:T(8,128)}, f32[256,256]{1,0:T(8,128)}, ...) | async-done | bytes 1310736 | tf_op jit(solution)/shard_map/psum | solution.py:44
  152.8 1.0 select_add_fusion
  153.8 0.1 copy.7
  153.9 0.8 copy-done.2
  154.8 11.7 %cholesky.49 = f32[128,128]{1,0:T(8,128)S(1)} custom-call(f32[128,128]{1,0:T(8,128)S(1)} %cholesky.115), custom_call_target="Cholesky" | custom-call | tf_op jit(solution)/shard_map/jit(cholesky)/cholesky | solution.py:47
  166.5 9.8 %custom-call.17 = f32[1,128,128]{1,2,0:T(8,128)S(1)} custom-call(f32[1,128,128]{2,1,0:T(8,128)S(1)} %get-tuple-element.61), custom_call_target="InvertDiagBlocksLowerTriangular" | custom-call | tf_op jit(solution)/shard_map/jit(cholesky)/cholesky | solution.py:47
  176.3 0.2 fusion.13
  176.5 0.3 convolution_subtract_fusion.1
  176.8 11.7 %cholesky.103 = f32[128,128]{1,0:T(8,128)S(1)} custom-call(f32[128,128]{1,0:T(8,128)S(1)} %convolution_subtract_fusion.1), custom_call_target="Cholesky" | custom-call | tf_op jit(solution)/shard_map/jit(cholesky)/cholesky | solution.py:47
  188.6 0.1 copy.10
  188.7 0.1 copy.9
  188.8 0.1 copy.8
  188.9 0.6 compare_reduce_fusion
  190.9 0.1 broadcast.150
  191.0 4.2 %while.5 = (s32[]{:T(128)}, f32[256,256]{0,1:T(8,128)S(1)}, s32[2,2]{1,0:T(2,128)S(1)}, f32[2,128,128]{2,1,0:T(8,128)S(1)}, s32[]{:T(128)}) while((s32[]{:T(128)}, f32[256,256]{0,1:T(8,128)S(1)}, s32[2,2]{1,0:T(2,128)S(1)}, f32[2,128,128]{2,1,0:T(8,128)S(1)}, s32[]{:T(128)}) %tuple.37), condition=%wide.while_cond, body=%wide.while_body.sunk | while | flops 2 | bytes 393321 | solution.py:27
  191.0 0.6 fusion.56
  191.6 1.4 dynamic-slice.12
  193.0 0.1 copy.18
  193.1 0.6 fusion.56
  193.7 1.4 dynamic-slice.12
  195.1 0.1 copy.18
  195.2 19.9 %custom-call.20 = f32[2,128,128]{1,2,0:T(8,128)S(1)} custom-call(f32[2,128,128]{2,1,0:T(8,128)S(1)} %get-tuple-element.27), custom_call_target="InvertDiagBlocksLowerTriangular" | custom-call | tf_op jit(solution)/shard_map/triangular_solve/custom-call.0 | solution.py:27
  215.1 0.3 fusion.11
  215.4 0.3 convolution_subtract_fusion
  215.8 0.3 fusion.16
  216.1 0.2 convolution_bitcast_fusion.4
  216.2 0.2 fusion.1
  216.4 0.2 convolution_bitcast_fusion.2
  216.6 0.2 fusion.33
  216.9 0.9 copy-done.3
  217.8 0.3 fusion.9
  218.1 0.3 fusion.17
  218.4 0.3 fusion.8
  218.8 0.8 copy.14
  219.6 0.6 subtract_select_fusion
  220.2 1.9 convolution_subtract_fusion.2
  222.1 1.9 dynamic-slice_subtract_fusion
  (31 shorter events, 0.4 us)
Async XLA Ops:
  7.2 96.1 %all-reduce.5.cloned.1.call-start = ((), (), s32[]{:S(2)}) async-start(), calls=%async_computation | async-start | bytes 2097152 | tf_op jit(solution)/shard_map/psum | solution.py:11
  8.4 1.2 copy-start
  8.4 144.4 %all-reduce.7.cloned.1.call-start = ((), (), s32[]{:S(2)}) async-start(), calls=%async_computation.1 | async-start | bytes 2621440 | tf_op jit(solution)/shard_map/psum | solution.py:44
  9.6 98.5 %collective-permute-start = (f32[256,1024]{1,0:T(8,128)S(1)}, f32[256,1024]{1,0:T(8,128)S(1)}, u32[]{:S(2)}, u32[]{:S(2)}) collective-permute-start(f32[256,1024]{1,0:T(8,128)S(1)} %copy-done), channel_id=1, source_target_pairs={{28,0},{0,4},{4,8},{8,12},{12,16},{16,20},{20,24},{24,28},{29,1},{... | collective-permute-start | bytes 3145736 | tf_op jit(solution)/shard_map/ppermute | solution.py:17
  103.3 3.1 %copy-start.1 = (f32[256,1024]{1,0:T(8,128)S(1)}, f32[256,1024]{1,0:T(8,128)}, u32[]{:S(2)}) copy-start(f32[256,1024]{1,0:T(8,128)} %all-reduce.5.cloned.1.call-done) | copy-start | bytes 3145732
  111.6 0.7 copy-start.5
  153.8 1.0 copy-start.2
  191.0 24.1 %copy-start.4 = (f32[256,256]{0,1:T(8,128)S(1)}, f32[256,256]{0,1:T(8,128)}, u32[]{:S(2)}) copy-start(f32[256,256]{0,1:T(8,128)} %get-tuple-element.53) | copy-start | bytes 786436
  216.8 1.0 copy-start.3
Sparse Core Ops, SparseCore 0:
  11.5 91.7 all-reduce.4
  111.7 41.0 all-reduce.6
where the time goes:
time: 234 us; the launch traced here: 231 us
  waiting for transfers between devices  117 us (50%)
  other arithmetic  56.7 us (24%)
  matrix products  17 us (7%)
  between operations  15.6 us (7%)
  blocking collectives  13.9 us (6%)
  local copies, waits for them, and re-layouts  9.07 us (4%)
    psum x1, waiting for transfers between devices, from_root(): return lax.psum(kept, axis)  90.7 us
    another operation x6, other arithmetic, on_device(): pivot_factor = jnp.linalg.cholesky(pivot_sum + ridge_shift * unit_full)  34 us
    psum x1, waiting for transfers between devices, on_device(): lax.psum((cross_part, self_part, cycle_part, pivot_part), 'par')  26.5 us
    another operation x5, other arithmetic, panel_solve(): lax.linalg.triangular_solve(pivot_factor, cross_tile, left_side=False, lo...  20 us
    psum x1, blocking collectives, from_root(): return lax.psum(kept, axis)  13.9 us
    dot_general x7, matrix products, kernel_tile(): jnp.dot(left_rows, right_rows.T, precision=lax.Precision.HIGHEST, preferr...  13.9 us
  transfers between devices with their start and end apart: 3, of which 2 were waited for; matrix products, arithmetic and copies ran while one was open for 3% of the time, Pallas kernels for 0%

commit v1 on v0

v1 whole, which is shorter than its diff:
```python
import functools

import jax
import jax.numpy as jnp
from jax import lax
from jax.experimental import pallas as pl
from jax.experimental.pallas import tpu as pltpu
from jax.sharding import PartitionSpec as P

ridge_shift = 0.05
MESH = pl.DeviceIdType.MESH
CHUNKS = 4
SELF, CROSS, PIVOT, CYCLE, BACK = range(5)


def dot_t(left, right):
    return lax.dot_general(
        left, right, (((1,), (1,)), ((), ())),
        precision=lax.Precision.HIGHEST, preferred_element_type=jnp.float32,
    )


def gather_kernel(
    nb, npar, a_ref, e_ref, full_ref, rows_ref, lead_e_ref,
    lead, prev, part, land1, land2,
    lead_send, lead_recv, e_send, e_recv, prev_send, prev_recv,
    rs_send, rs_recv, ag_send, ag_recv,
):
    b = lax.axis_index("blk")
    j = lax.axis_index("par")
    size = a_ref.shape[0]
    half = size // 2
    step = half // CHUNKS
    share = size // npar
    odd = lax.rem(b, 2)
    sib = b + 1 - 2 * odd
    nxt, prv = lax.rem(b + 1, nb), lax.rem(b + nb - 1, nb)

    def to_blk(src, dst, send, recv, target):
        return pltpu.make_async_remote_copy(
            src_ref=src, dst_ref=dst, send_sem=send, recv_sem=recv,
            device_id=(target, j), device_id_type=MESH,
        )

    def to_par(src, dst, send, recv, target):
        return pltpu.make_async_remote_copy(
            src_ref=src, dst_ref=dst, send_sem=send, recv_sem=recv,
            device_id=(b, target), device_id_type=MESH,
        )

    barrier = pltpu.get_barrier_semaphore()

    def greet(row, col):
        pl.semaphore_signal(barrier, inc=1, device_id=(row, col), device_id_type=MESH)

    greet(nxt, j)
    greet(prv, j)
    for d in range(1, npar):
        greet(b, lax.rem(j + d, npar))

    @pl.when(b + 2 < nb)
    def _():
        greet(b + 2, j)

    @pl.when(b >= 2)
    def _():
        greet(b - 2, j)

    outer = (b + 2 < nb).astype(jnp.int32) + (b >= 2).astype(jnp.int32)
    pl.semaphore_wait(barrier, 2 + npar - 1 + outer)

    def piece(h, c):
        return pl.ds(pl.multiple_of(h * half + c * step, step), step)

    def lead_copy(src_ref, h, c, kind, target):
        at = piece(h, c)
        return to_blk(
            src_ref.at[at], lead.at[at], lead_send.at[kind, c], lead_recv.at[h, c], target
        )

    main = 1 - odd

    @pl.when(b == 0)
    def _():
        for c in range(CHUNKS):
            lead_copy(a_ref, 0, c, 2, 1).start()
            if nb > 2:
                lead_copy(a_ref, 1, c, 0, 2).start()
        to_blk(e_ref, lead_e_ref, e_send.at[1], e_recv, 1).start()
        if nb > 2:
            to_blk(e_ref, lead_e_ref, e_send.at[0], e_recv, 2).start()
        for c in range(CHUNKS):
            lead_copy(a_ref, 1, c, 1, 1).start()

    prev_copy = to_blk(a_ref, prev, prev_send, prev_recv, nxt)

    @pl.when(b != 0)
    def _():
        prev_copy.start()

    part[SELF] = dot_t(a_ref[...], a_ref[...])

    @pl.when(b == 0)
    def _():
        part[CROSS] = part[SELF]
        part[PIVOT] = part[SELF]
        lead_e_ref[...] = e_ref[...]

    @pl.when(b != 0)
    def _():
        for c in range(CHUNKS):
            lead_copy(lead, main, c, 0, b).wait_recv()

            @pl.when(b + 2 < nb)
            def _():
                lead_copy(lead, main, c, 0, b + 2).start()

            @pl.when(b > 1)
            def _():
                lead_copy(lead, main, c, 1, sib).start()

        to_blk(lead_e_ref, lead_e_ref, e_send.at[0], e_recv, b).wait_recv()

        @pl.when(odd == 0)
        def _():
            to_blk(lead_e_ref, lead_e_ref, e_send.at[1], e_recv, b + 1).start()

            @pl.when(b + 2 < nb)
            def _():
                to_blk(lead_e_ref, lead_e_ref, e_send.at[0], e_recv, b + 2).start()

        for c in range(CHUNKS):
            lead_copy(lead, 1 - main, c, 0, b).wait_recv()
        part[CROSS] = dot_t(a_ref[...], lead[...])
        part[PIVOT] = dot_t(lead[...], lead[...])

    def rows_of(p):
        return pl.ds(pl.multiple_of(p * share, share), share)

    def scatter(d, phase):
        p = lax.rem(j + d, npar)
        low, high = ((SELF, PIVOT + 1), (CYCLE, BACK + 1))[phase]
        land = (land1, land2)[phase]
        return to_par(
            part.at[pl.ds(low, high - low), rows_of(p)], land.at[d - 1],
            rs_send.at[phase, d - 1], rs_recv.at[phase, d - 1], p,
        )

    def gather(d, phase):
        low, count = ((0, 2), (2, 1))[phase]
        mine = full_ref.at[pl.ds(low, count), rows_of(j)]
        return to_par(
            mine, mine, ag_send.at[phase, d - 1], ag_recv.at[phase, d - 1],
            lax.rem(j + d, npar),
        )

    def gathered(d, phase):
        low, count = ((0, 2), (2, 1))[phase]
        theirs = full_ref.at[pl.ds(low, count), rows_of(lax.rem(j + npar - d, npar))]
        return to_par(
            theirs, theirs, ag_send.at[phase, d - 1], ag_recv.at[phase, d - 1],
            lax.rem(j + d, npar),
        )

    peers = range(1, npar)
    for d in peers:
        scatter(d, 0).start()

    @pl.when(b == 1)
    def _():
        part[CYCLE] = part[CROSS]
        part[BACK] = part[PIVOT]

    @pl.when(jnp.logical_and(b != 1, b != 0))
    def _():
        prev_copy.wait_recv()
        part[CYCLE] = dot_t(a_ref[...], prev[...])
        part[BACK] = dot_t(prev[...], lead[...])

    @pl.when(b == 0)
    def _():
        prev_copy.wait_recv()
        part[CYCLE] = dot_t(a_ref[...], prev[...])
        part[BACK] = dot_t(prev[...], a_ref[...])

    for d in peers:
        scatter(d, 1).start()
    mine = rows_of(j)

    for d in peers:
        scatter(d, 0).wait_recv()

    def total(t, land, slot):
        value = part[t, mine]
        for d in peers:
            value = value + land[d - 1, slot]
        return value

    rows_ref[0] = total(SELF, land1, 0)
    full_ref[0, mine] = total(PIVOT, land1, 2)
    full_ref[1, mine] = total(CROSS, land1, 1)
    for d in peers:
        gather(d, 0).start()
    for d in peers:
        scatter(d, 1).wait_recv()
    full_ref[2, mine] = total(BACK, land2, 1)
    for d in peers:
        gather(d, 1).start()
    rows_ref[1] = total(CYCLE, land2, 0)

    for phase in range(2):
        for d in peers:
            gathered(d, phase).wait_recv()
    for phase in range(2):
        for d in peers:
            scatter(d, phase).wait_send()
            gather(d, phase).wait_send()

    @pl.when(b != 0)
    def _():
        prev_copy.wait_send()
        for c in range(CHUNKS):
            @pl.when(b + 2 < nb)
            def _():
                lead_copy(lead, main, c, 0, b + 2).wait_send()

            @pl.when(b > 1)
            def _():
                lead_copy(lead, main, c, 1, sib).wait_send()

        @pl.when(odd == 0)
        def _():
            to_blk(lead_e_ref, lead_e_ref, e_send.at[1], e_recv, b + 1).wait_send()

            @pl.when(b + 2 < nb)
            def _():
                to_blk(lead_e_ref, lead_e_ref, e_send.at[0], e_recv, b + 2).wait_send()

    @pl.when(b == 0)
    def _():
        for c in range(CHUNKS):
            lead_copy(a_ref, 0, c, 2, 1).wait_send()
            lead_copy(a_ref, 1, c, 1, 1).wait_send()
            if nb > 2:
                lead_copy(a_ref, 1, c, 0, 2).wait_send()
        to_blk(e_ref, lead_e_ref, e_send.at[1], e_recv, 1).wait_send()
        if nb > 2:
            to_blk(e_ref, lead_e_ref, e_send.at[0], e_recv, 2).wait_send()


def inverse_factor(tile):
    n = tile.shape[0]
    row_id = lax.broadcasted_iota(jnp.int32, (n, n), 0)
    col_id = lax.broadcasted_iota(jnp.int32, (n, n), 1)
    unit = (row_id == col_id).astype(jnp.float32)
    left = [tile[i * 8:(i + 1) * 8] for i in range(n // 8)]
    right = [unit[i * 8:(i + 1) * 8] for i in range(n // 8)]
    sub = lax.broadcasted_iota(jnp.int32, (8, 1), 0)
    for k in range(n):
        g, s = divmod(k, 8)
        row = left[g][s:s + 1]
        row_right = right[g][s:s + 1]
        inv = 1.0 / row[:, k:k + 1]
        row, row_right = row * inv, row_right * inv
        for i in range(g, n // 8):
            col = left[i][:, k:k + 1]
            if i == g:
                if s == 7:
                    continue
                col = jnp.where(sub > s, col, 0.0)
            left[i] = left[i] - col * row
            right[i] = right[i] - col * row_right
    left, right = jnp.concatenate(left, 0), jnp.concatenate(right, 0)
    pivots = jnp.sum(left * unit, axis=1, keepdims=True)
    return right * lax.rsqrt(pivots)


def factor_kernel(
    place_ref, full_ref, rows_ref, lead_e_ref, e_ref,
    panel_ref, e_next_ref, diag_ref, near_ref, prev_panel,
):
    size = e_ref.shape[1]
    share = rows_ref.shape[1]
    bs = size // 2
    unit = (
        lax.broadcasted_iota(jnp.int32, (bs, bs), 0) == lax.broadcasted_iota(jnp.int32, (bs, bs), 1)
    ).astype(jnp.float32) * ridge_shift
    inv0 = inverse_factor(full_ref[0, :bs, :bs] + unit)
    below = jnp.concatenate(
        [full_ref[0, bs:, :bs], full_ref[1, :, :bs], full_ref[2, :, :bs], lead_e_ref[:, :bs]], 0
    )
    rest = jnp.concatenate(
        [full_ref[0, bs:, bs:] + unit, full_ref[1, :, bs:], full_ref[2, :, bs:], lead_e_ref[:, bs:]], 0
    )
    first = dot_t(below, inv0)
    rest = rest - dot_t(first, first[:bs])
    inv1 = inverse_factor(rest[:bs])
    second = dot_t(rest[bs:], inv1)
    panel_ref[:, :bs] = first[bs:bs + size]
    panel_ref[:, bs:] = second[:size]
    prev_panel[:, :bs] = first[bs + size:bs + 2 * size]
    prev_panel[:, bs:] = second[size:2 * size]
    lead_row = jnp.concatenate([first[bs + 2 * size:], second[2 * size:]], 1)
    panel = panel_ref[...]
    remainder = e_ref[...] - dot_t(lead_row, panel)
    e_next_ref[...] = jnp.where(place_ref[0] == 0, lead_row, remainder)
    start = pl.multiple_of(place_ref[1] * share, share)
    part = panel_ref[pl.ds(start, share)]
    shift = jnp.where(
        lax.broadcasted_iota(jnp.int32, (share, size), 0) + start
        == lax.broadcasted_iota(jnp.int32, (share, size), 1),
        ridge_shift, 0.0,
    )
    diag_ref[...] = rows_ref[0] + shift - dot_t(part, panel)
    near_ref[...] = rows_ref[1] - dot_t(part, prev_panel[...])


def on_device(nb, npar, log_derivs, energies):
    size, depth = log_derivs.shape
    share = size // npar
    f32 = jnp.float32
    vmem = pl.BlockSpec(memory_space=pltpu.VMEM)
    e_rows = jnp.broadcast_to(energies[None], (8, size))
    dma = pltpu.SemaphoreType.DMA
    full, rows, lead_e = pl.pallas_call(
        functools.partial(gather_kernel, nb, npar),
        out_shape=(
            jax.ShapeDtypeStruct((3, size, size), f32),
            jax.ShapeDtypeStruct((2, share, size), f32),
            jax.ShapeDtypeStruct((8, size), f32),
        ),
        in_specs=[vmem, vmem],
        out_specs=(vmem, vmem, vmem),
        scratch_shapes=[
            pltpu.VMEM((size, depth), f32),
            pltpu.VMEM((size, depth), f32),
            pltpu.VMEM((5, size, size), f32),
            pltpu.VMEM((npar - 1, 3, share, size), f32),
            pltpu.VMEM((npar - 1, 2, share, size), f32),
            dma((3, CHUNKS)), dma((2, CHUNKS)), dma((2,)), dma, dma, dma,
            dma((2, npar - 1)), dma((2, npar - 1)), dma((2, npar - 1)), dma((2, npar - 1)),
        ],
        compiler_params=pltpu.CompilerParams(
            collective_id=0, has_side_effects=True, vmem_limit_bytes=40 * 2**20
        ),
        name="gather_tiles",
    )(log_derivs, e_rows)
    place = jnp.stack([lax.axis_index("blk"), lax.axis_index("par")]).astype(jnp.int32)
    panel, e_next, diag, near = pl.pallas_call(
        factor_kernel,
        out_shape=(
            jax.ShapeDtypeStruct((size, size), f32),
            jax.ShapeDtypeStruct((8, size), f32),
            jax.ShapeDtypeStruct((share, size), f32),
            jax.ShapeDtypeStruct((share, size), f32),
        ),
        in_specs=[pl.BlockSpec(memory_space=pltpu.SMEM), vmem, vmem, vmem, vmem],
        out_specs=(vmem, vmem, vmem, vmem),
        scratch_shapes=[pltpu.VMEM((size, size), f32)],
        compiler_params=pltpu.CompilerParams(vmem_limit_bytes=40 * 2**20),
        name="factor_tiles",
    )(place, full, rows, lead_e, e_rows)
    return panel, e_next[0], diag, near


def solution(mesh):
    nb, npar = mesh.shape["blk"], mesh.shape["par"]
    return jax.shard_map(
        functools.partial(on_device, nb, npar),
        mesh=mesh,
        in_specs=(P("blk", "par"), P("blk")),
        out_specs=(P("blk", None), P("blk"), P(("blk", "par"), None), P(("blk", "par"), None)),
        check_vma=False,
    )
```

time: 234 us -> 105 us (0.45); the launches traced: 231 us -> 105 us
  waiting for transfers between devices: 117 us -> 0 us
  Pallas kernels: 0 us -> 101 us
  other arithmetic: 56.7 us -> 0.08 us
  matrix products: 17 us -> 0 us
  between operations: 15.6 us -> 0.65 us
  blocking collectives: 13.9 us -> 0 us
  local copies, waits for them, and re-layouts: 9.07 us -> 2.38 us
    psum x2 -> x0, waiting for transfers between devices: 117 us -> none  [the longest x1 90.7 us: from_root(): return lax.psum(kept, axis)]
    pallas_call x0 -> x2, Pallas kernels: none -> 101 us  [the longest x1 74.7 us: on_device(): pl.pallas_call(functools.partial(gather_kernel, nb, npar), out_shape=(jax...]
    another operation x12 -> x1, other arithmetic: 53.9 us -> 0.08 us  [on_device(): jnp.stack([lax.axis_index('blk'), lax.axis_index('par')]).astype(jnp.int32)]
    dot_general x8 -> x0, matrix products: 14.1 us -> none  [the longest x7 13.9 us: kernel_tile(): jnp.dot(left_rows, right_rows.T, precision=lax.Precision.HIGHEST, preferr...]
    psum x1 -> x0, blocking collectives: 13.9 us -> none  [from_root(): return lax.psum(kept, axis)]
    another operation x18 -> x0, local copies, waits for them, and re-layouts: 4.54 us -> none  [the longest x11 4.22 us: panel_solve(): lax.linalg.triangular_solve(pivot_factor, cross_tile, left_side=False, lo...]
    another operation x11 -> x0, matrix products: 2.85 us -> none  [the longest x6 1.88 us: panel_solve(): lax.linalg.triangular_solve(pivot_factor, cross_tile, left_side=False, lo...]
    unnamed x13 -> x4, local copies, waits for them, and re-layouts: 4.41 us -> 1.82 us
  transfers between devices with their start and end apart: 3 -> 0, of which waited for: 2 -> 0; matrix products, arithmetic and copies ran while one was open for 3% -> 0% of each run, Pallas kernels for 0% -> 0%
where the time goes in v1:
time: 105 us
  Pallas kernels  101 us (96%)
  local copies, waits for them, and re-layouts  2.38 us (2%)
    pallas_call x1, Pallas kernels, on_device(): pl.pallas_call(functools.partial(gather_kernel, nb, npar), out_shape=(jax...  74.7 us
    pallas_call x1, Pallas kernels, on_device(): pl.pallas_call(factor_kernel, out_shape=(jax.ShapeDtypeStruct((size, size...  26.7 us

profile of v1, /device:TPU:27, one launch (start us, length us, event | category | flops | bytes accessed | tf_op | source)
XLA Modules:
  0.0 104.6 jit_solution(13248601384056728019)
XLA Ops:
  0.6 0.0 copy-start.1
  0.6 0.1 pad_add_fusion.place_ref
  0.7 0.6 copy-done.1
  1.3 0.0 copy-start
  1.3 1.2 %copy-done = f32[256,1024]{1,0:T(8,128)S(1)} copy-done((f32[256,1024]{1,0:T(8,128)S(1)}, f32[256,1024]{1,0:T(8,128)}, u32[]{:S(2)}) %copy-start) | copy-done | bytes 1048600
  2.5 74.7 %gather_tiles.1 = (f32[3,256,256]{2,1,0:T(8,128)S(1)}, f32[2,64,256]{2,1,0:T(8,128)S(1)}, f32[8,256]{1,0:T(8,128)S(1)}) custom-call(f32[256,1024]{1,0:T(8,128)S(1)} %copy-done, f32[8,256]{1,0:T(8,128)S(1)} %broadcast_in_dim.2.e_ref), custom_call_target="tpu_custom_call" | custom-call | tf_op jit(solution)/shard_map/gather_tiles/pallas_call | solution.py:325
  77.3 26.7 %factor_tiles.1 = (f32[256,256]{1,0:T(8,128)}, f32[8,256]{1,0:T(8,128)S(1)}, f32[64,256]{1,0:T(8,128)}, f32[64,256]{1,0:T(8,128)}) custom-call(s32[2]{0:T(128)S(1)} %pad_add_fusion.place_ref, f32[3,256,256]{2,1,0:T(8,128)S(1)} %get-tuple-element.11.full_ref, f32[2,64,256]{2,1,0:T(8,128)S(1)} %get-tuple-element.12.rows_ref, ...), custom_call_target="tpu_custom_call" | custom-call | tf_op jit(solution)/shard_map/factor_tiles/pallas_call | solution.py:349
  104.0 0.6 slice.3
  (1 shorter events, 0.0 us)
Async XLA Ops:
  0.6 0.7 copy-start.1
  1.3 1.2 %copy-start = (f32[256,1024]{1,0:T(8,128)S(1)}, f32[256,1024]{1,0:T(8,128)}, u32[]{:S(2)}) copy-start(f32[256,1024]{1,0:T(8,128)} %a_ref.1) | copy-start | bytes 3145732

commit v2 on v1

v2 whole, which is shorter than its diff:
```python
import functools

import jax
import jax.numpy as jnp
from jax import lax
from jax.experimental import pallas as pl
from jax.experimental.pallas import tpu as pltpu
from jax.sharding import PartitionSpec as P

ridge_shift = 0.05
MESH = pl.DeviceIdType.MESH
CHUNKS = 4
PREV_CHUNKS = 4
SELF, CROSS, CYCLE = range(3)
LEFT, BACK = range(2)


def dot_t(left, right):
    return lax.dot_general(
        left, right, (((1,), (1,)), ((), ())),
        precision=lax.Precision.HIGHEST, preferred_element_type=jnp.float32,
    )


def tile_kernel(
    nb, npar, a_ref, e_ref, panel_ref, e_next_ref, diag_ref, near_ref,
    lead, prev, part, land, full, fac, back_panel,
    lead_send, lead_recv, fac_send, fac_recv, share_send, share_recv,
    prev_send, prev_recv, rs_send, rs_recv, ag_send, ag_recv, back_send, back_recv,
):
    b = lax.axis_index("blk")
    j = lax.axis_index("par")
    size = a_ref.shape[0]
    half = size // 2
    step = half // CHUNKS
    share = size // npar
    bs = half
    odd = lax.rem(b, 2)
    sib = b + 1 - 2 * odd
    nxt, prv = lax.rem(b + 1, nb), lax.rem(b + nb - 1, nb)
    peers = range(1, npar)

    def to_blk(src, dst, send, recv, target):
        return pltpu.make_async_remote_copy(
            src_ref=src, dst_ref=dst, send_sem=send, recv_sem=recv,
            device_id=(target, j), device_id_type=MESH,
        )

    def to_par(src, dst, send, recv, target):
        return pltpu.make_async_remote_copy(
            src_ref=src, dst_ref=dst, send_sem=send, recv_sem=recv,
            device_id=(b, target), device_id_type=MESH,
        )

    barrier = pltpu.get_barrier_semaphore()

    def greet(row, col):
        pl.semaphore_signal(barrier, inc=1, device_id=(row, col), device_id_type=MESH)

    greet(nxt, j)
    greet(prv, j)
    for d in range(1, npar):
        greet(b, lax.rem(j + d, npar))

    @pl.when(b + 2 < nb)
    def _():
        greet(b + 2, j)

    @pl.when(b >= 2)
    def _():
        greet(b - 2, j)

    outer = (b + 2 < nb).astype(jnp.int32) + (b >= 2).astype(jnp.int32)
    pl.semaphore_wait(barrier, 2 + npar - 1 + outer)

    def piece(h, c):
        return pl.ds(pl.multiple_of(h * half + c * step, step), step)

    def lead_copy(src_ref, h, c, kind, target):
        at = piece(h, c)
        return to_blk(
            src_ref.at[at], lead.at[at], lead_send.at[kind, c], lead_recv.at[h, c], target
        )

    main = 1 - odd

    @pl.when(b == 0)
    def _():
        for c in range(CHUNKS):
            lead_copy(a_ref, 0, c, 2, 1).start()
            if nb > 2:
                lead_copy(a_ref, 1, c, 0, 2).start()
        for c in range(CHUNKS):
            lead_copy(a_ref, 1, c, 1, 1).start()

    prev_step = size // PREV_CHUNKS

    def prev_copy(q):
        at = pl.ds(q * prev_step, prev_step)
        return to_blk(a_ref.at[at], prev.at[at], prev_send.at[q], prev_recv.at[q], nxt)

    def rows_of(p, count):
        return pl.ds(pl.multiple_of(p * count, 8), count)

    mine = rows_of(j, share)

    def scatter(d, t):
        p = lax.rem(j + d, npar)
        return to_par(
            part.at[t, rows_of(p, share)], land.at[t, d - 1],
            rs_send.at[t, d - 1], rs_recv.at[t, d - 1], p,
        )

    def total(t):
        value = part[t, mine]
        for d in peers:
            scatter(d, t).wait_recv()
            value = value + land[t, d - 1]
        return value

    def gather(d, t, owner):
        at = full.at[t, rows_of(owner, share)]
        return to_par(at, at, ag_send.at[t, d - 1], ag_recv.at[t, d - 1], lax.rem(j + d, npar))

    def wait_gathered(t):
        for d in peers:
            gather(d, t, lax.rem(j + npar - d, npar)).wait_recv()

    fac_share = fac.shape[0] // npar

    def pass_fac(kind, target):
        at = fac.at[rows_of(j, fac_share)]
        return to_blk(at, at, fac_send.at[kind], fac_recv, target)

    def share_fac(d, owner):
        at = fac.at[rows_of(owner, fac_share)]
        return to_par(at, at, share_send.at[d - 1], share_recv.at[d - 1], lax.rem(j + d, npar))

    def back_copy():
        return to_blk(full.at[LEFT, mine], full.at[BACK, mine], back_send, back_recv, nxt)

    @pl.when(b != 0)
    def _():
        for q in range(PREV_CHUNKS // 2):
            prev_copy(q).start()

    part[SELF] = dot_t(a_ref[...], a_ref[...])

    @pl.when(b == 0)
    def _():
        part[CROSS] = part[SELF]

    @pl.when(b != 0)
    def _():
        for d in peers:
            scatter(d, SELF).start()
        for c in range(CHUNKS):
            lead_copy(lead, main, c, 0, b).wait_recv()

            @pl.when(b + 2 < nb)
            def _():
                lead_copy(lead, main, c, 0, b + 2).start()

            @pl.when(b > 1)
            def _():
                lead_copy(lead, main, c, 1, sib).start()

            if c % 2 == 1:
                prev_copy(PREV_CHUNKS // 2 + c // 2).start()
        for c in range(CHUNKS):
            lead_copy(lead, 1 - main, c, 0, b).wait_recv()
        part[CROSS] = dot_t(a_ref[...], lead[...])

    for d in peers:
        scatter(d, CROSS).start()

    @pl.when(b == 0)
    def _():
        for d in peers:
            scatter(d, SELF).start()

    full[LEFT, mine] = total(CROSS)
    for d in peers:
        gather(d, LEFT, j).start()
    back_copy().start()

    @pl.when(b == 0)
    def _():
        wait_gathered(LEFT)
        unit = (
            lax.broadcasted_iota(jnp.int32, (bs, bs), 0)
            == lax.broadcasted_iota(jnp.int32, (bs, bs), 1)
        ).astype(jnp.float32) * ridge_shift
        inv0 = inverse_factor(full[LEFT, :bs, :bs] + unit)
        low = dot_t(full[LEFT, bs:, :bs], inv0)
        inv1 = inverse_factor(full[LEFT, bs:, bs:] + unit - dot_t(low, low))
        lead0 = dot_t(e_ref[:, :bs], inv0)
        lead1 = dot_t(e_ref[:, bs:] - dot_t(lead0, low), inv1)
        fac[0:bs] = inv0
        fac[bs:2 * bs] = low
        fac[2 * bs:3 * bs] = inv1
        fac[3 * bs:3 * bs + 8] = lead0
        fac[3 * bs + 8:3 * bs + 16] = lead1
        fac[3 * bs + 16:] = jnp.zeros((fac.shape[0] - 3 * bs - 16, bs), jnp.float32)
        pass_fac(1, 1).start()
        if nb > 2:
            pass_fac(0, 2).start()

    @pl.when(b != 0)
    def _():
        pass_fac(0, b).wait_recv()

        @pl.when(odd == 0)
        def _():
            pass_fac(1, b + 1).start()

            @pl.when(b + 2 < nb)
            def _():
                pass_fac(0, b + 2).start()

        for d in peers:
            share_fac(d, j).start()

    diag = total(SELF)
    back_copy().wait_recv()
    for d in peers:
        gather(d, BACK, j).start()

    @pl.when(b == 1)
    def _():
        part[CYCLE] = part[CROSS]

    @pl.when(b != 1)
    def _():
        for q in range(PREV_CHUNKS):
            prev_copy(q).wait_recv()
        part[CYCLE] = dot_t(a_ref[...], prev[...])

    for d in peers:
        scatter(d, CYCLE).start()

    @pl.when(b != 0)
    def _():
        wait_gathered(LEFT)
        for d in peers:
            share_fac(d, lax.rem(j + npar - d, npar)).wait_recv()

    def solve(t, out):
        first = dot_t(full[t, :, :bs], fac[0:bs])
        second = full[t, :, bs:] - dot_t(first, fac[bs:2 * bs])
        out[:, :bs] = first
        out[:, bs:] = dot_t(second, fac[2 * bs:3 * bs])

    solve(LEFT, panel_ref)
    lead_row = jnp.concatenate([fac[3 * bs:3 * bs + 8], fac[3 * bs + 8:3 * bs + 16]], 1)
    panel = panel_ref[...]
    remainder = e_ref[...] - dot_t(lead_row, panel)
    e_next_ref[...] = jnp.where(b == 0, lead_row, remainder)
    panel_rows = panel_ref[mine]
    shift = jnp.where(
        lax.broadcasted_iota(jnp.int32, (share, size), 0) + j * share
        == lax.broadcasted_iota(jnp.int32, (share, size), 1),
        ridge_shift, 0.0,
    )
    diag_ref[...] = diag + shift - dot_t(panel_rows, panel)
    wait_gathered(BACK)
    solve(BACK, back_panel)
    taken = dot_t(panel_rows, back_panel[...])
    near_ref[...] = total(CYCLE) - taken

    for d in peers:
        for t in (SELF, CROSS, CYCLE):
            scatter(d, t).wait_send()
        for t in (LEFT, BACK):
            gather(d, t, j).wait_send()
    back_copy().wait_send()

    @pl.when(b != 0)
    def _():
        for q in range(PREV_CHUNKS):
            prev_copy(q).wait_send()
        for d in peers:
            share_fac(d, j).wait_send()
        for c in range(CHUNKS):
            @pl.when(b + 2 < nb)
            def _():
                lead_copy(lead, main, c, 0, b + 2).wait_send()

            @pl.when(b > 1)
            def _():
                lead_copy(lead, main, c, 1, sib).wait_send()

        @pl.when(odd == 0)
        def _():
            pass_fac(1, b + 1).wait_send()

            @pl.when(b + 2 < nb)
            def _():
                pass_fac(0, b + 2).wait_send()

    @pl.when(b == 0)
    def _():
        for c in range(CHUNKS):
            lead_copy(a_ref, 0, c, 2, 1).wait_send()
            lead_copy(a_ref, 1, c, 1, 1).wait_send()
            if nb > 2:
                lead_copy(a_ref, 1, c, 0, 2).wait_send()
        pass_fac(1, 1).wait_send()
        if nb > 2:
            pass_fac(0, 2).wait_send()


def inverse_factor(tile):
    n = tile.shape[0]
    row_id = lax.broadcasted_iota(jnp.int32, (n, n), 0)
    col_id = lax.broadcasted_iota(jnp.int32, (n, n), 1)
    unit = (row_id == col_id).astype(jnp.float32)
    left = [tile[i * 8:(i + 1) * 8] for i in range(n // 8)]
    right = [unit[i * 8:(i + 1) * 8] for i in range(n // 8)]
    sub = lax.broadcasted_iota(jnp.int32, (8, 1), 0)
    for k in range(n):
        g, s = divmod(k, 8)
        row = left[g][s:s + 1]
        row_right = right[g][s:s + 1]
        inv = 1.0 / row[:, k:k + 1]
        row, row_right = row * inv, row_right * inv
        for i in range(g, n // 8):
            col = left[i][:, k:k + 1]
            if i == g:
                if s == 7:
                    continue
                col = jnp.where(sub > s, col, 0.0)
            left[i] = left[i] - col * row
            right[i] = right[i] - col * row_right
    left, right = jnp.concatenate(left, 0), jnp.concatenate(right, 0)
    pivots = jnp.sum(left * unit, axis=1, keepdims=True)
    return right * lax.rsqrt(pivots)


def on_device(nb, npar, log_derivs, energies):
    size, depth = log_derivs.shape
    share = size // npar
    fac_rows = ((3 * (size // 2) + 16) // (8 * npar) + 1) * 8 * npar
    f32 = jnp.float32
    vmem = pl.BlockSpec(memory_space=pltpu.VMEM)
    e_rows = jnp.broadcast_to(energies[None], (8, size))
    dma = pltpu.SemaphoreType.DMA
    panel, e_next, diag, near = pl.pallas_call(
        functools.partial(tile_kernel, nb, npar),
        out_shape=(
            jax.ShapeDtypeStruct((size, size), f32),
            jax.ShapeDtypeStruct((8, size), f32),
            jax.ShapeDtypeStruct((share, size), f32),
            jax.ShapeDtypeStruct((share, size), f32),
        ),
        in_specs=[vmem, vmem],
        out_specs=(vmem, vmem, vmem, vmem),
        scratch_shapes=[
            pltpu.VMEM((size, depth), f32),
            pltpu.VMEM((size, depth), f32),
            pltpu.VMEM((3, size, size), f32),
            pltpu.VMEM((3, npar - 1, share, size), f32),
            pltpu.VMEM((2, size, size), f32),
            pltpu.VMEM((fac_rows, size // 2), f32),
            pltpu.VMEM((size, size), f32),
            dma((3, CHUNKS)), dma((2, CHUNKS)), dma((2,)), dma,
            dma((npar - 1,)), dma((npar - 1,)), dma((PREV_CHUNKS,)), dma((PREV_CHUNKS,)),
            dma((3, npar - 1)), dma((3, npar - 1)), dma((2, npar - 1)), dma((2, npar - 1)),
            dma, dma,
        ],
        compiler_params=pltpu.CompilerParams(
            collective_id=0, has_side_effects=True, vmem_limit_bytes=40 * 2**20
        ),
        name="all_tiles",
    )(log_derivs, e_rows)
    return panel, e_next[0], diag, near


def solution(mesh):
    nb, npar = mesh.shape["blk"], mesh.shape["par"]
    return jax.shard_map(
        functools.partial(on_device, nb, npar),
        mesh=mesh,
        in_specs=(P("blk", "par"), P("blk")),
        out_specs=(P("blk", None), P("blk"), P(("blk", "par"), None), P(("blk", "par"), None)),
        check_vma=False,
    )
```

time: 105 us -> 74.5 us (0.71)
  Pallas kernels: 101 us -> 68.2 us
  local copies, waits for them, and re-layouts: 2.38 us -> 4.43 us
    pallas_call x2 -> x1, Pallas kernels: 101 us -> 68.2 us  [on_device(): pl.pallas_call(functools.partial(tile_kernel, nb, npar), out_shape=(jax.S...]
    unnamed x4 -> x5, local copies, waits for them, and re-layouts: 1.82 us -> 3.18 us
where the time goes in v2:
time: 74.5 us; the launch traced here: 73.3 us
  Pallas kernels  68.2 us (92%)
  local copies, waits for them, and re-layouts  4.43 us (6%)
    pallas_call x1, Pallas kernels, on_device(): pl.pallas_call(functools.partial(tile_kernel, nb, npar), out_shape=(jax.S...  68.2 us
    unnamed x5, local copies, waits for them, and re-layouts  3.18 us

profile of v2, /device:TPU:27, one launch (start us, length us, event | category | flops | bytes accessed | tf_op | source)
XLA Modules:
  0.0 73.3 jit_solution(14835102442651677057)
XLA Ops:
  0.6 0.7 broadcast_in_dim.2.e_ref
  1.3 0.0 copy-start
  1.3 1.2 %copy-done = f32[256,1024]{1,0:T(8,128)S(1)} copy-done((f32[256,1024]{1,0:T(8,128)S(1)}, f32[256,1024]{1,0:T(8,128)}, u32[]{:S(2)}) %copy-start) | copy-done | bytes 1048600
  2.5 68.2 %all_tiles.1 = (f32[256,256]{1,0:T(8,128)S(1)}, f32[8,256]{1,0:T(8,128)S(1)}, f32[64,256]{1,0:T(8,128)S(1)}, f32[64,256]{1,0:T(8,128)S(1)}) custom-call(f32[256,1024]{1,0:T(8,128)S(1)} %copy-done, f32[8,256]{1,0:T(8,128)S(1)} %broadcast_in_dim.2.e_ref), custom_call_target="tpu_custom_call" | custom-call | tf_op jit(solution)/shard_map/all_tiles/pallas_call | solution.py:348
  70.8 0.6 slice.3
  71.3 0.7 copy.9
  72.0 0.6 copy.10
  72.7 0.6 copy.11
Async XLA Ops:
  1.3 1.2 %copy-start = (f32[256,1024]{1,0:T(8,128)S(1)}, f32[256,1024]{1,0:T(8,128)}, u32[]{:S(2)}) copy-start(f32[256,1024]{1,0:T(8,128)} %a_ref.1) | copy-start | bytes 3145732

commit v3 on v2

--- a/solution.py
+++ b/solution.py
@@ -9,8 +9,9 @@
 
 ridge_shift = 0.05
 MESH = pl.DeviceIdType.MESH
-CHUNKS = 4
-PREV_CHUNKS = 4
+CHUNKS = 16
+PREV_CHUNKS = 8
+PREV_EARLY = 4
 SELF, CROSS, CYCLE = range(3)
 LEFT, BACK = range(2)
 
@@ -90,8 +91,9 @@
             lead_copy(a_ref, 0, c, 2, 1).start()
             if nb > 2:
                 lead_copy(a_ref, 1, c, 0, 2).start()
-        for c in range(CHUNKS):
-            lead_copy(a_ref, 1, c, 1, 1).start()
+        if nb <= 2:
+            for c in range(CHUNKS):
+                lead_copy(a_ref, 1, c, 1, 1).start()
 
     prev_step = size // PREV_CHUNKS
 
@@ -141,7 +143,7 @@
 
     @pl.when(b != 0)
     def _():
-        for q in range(PREV_CHUNKS // 2):
+        for q in range(PREV_EARLY):
             prev_copy(q).start()
 
     part[SELF] = dot_t(a_ref[...], a_ref[...])
@@ -165,10 +167,21 @@
             def _():
                 lead_copy(lead, main, c, 1, sib).start()
 
-            if c % 2 == 1:
-                prev_copy(PREV_CHUNKS // 2 + c // 2).start()
-        for c in range(CHUNKS):
-            lead_copy(lead, 1 - main, c, 0, b).wait_recv()
+            @pl.when(b == 3)
+            def _():
+                lead_copy(lead, 1, c, 0, b).wait_recv()
+                lead_copy(lead, 1, c, 2, 1).start()
+
+            late = PREV_CHUNKS - PREV_EARLY
+            for q in range(late):
+                if c == (q + 1) * CHUNKS // late - 1:
+                    prev_copy(PREV_EARLY + q).start()
+
+        @pl.when(b != 3)
+        def _():
+            for c in range(CHUNKS):
+                lead_copy(lead, 1 - main, c, 0, b).wait_recv()
+
         part[CROSS] = dot_t(a_ref[...], lead[...])
 
     for d in peers:
@@ -290,6 +303,10 @@
             def _():
                 lead_copy(lead, main, c, 1, sib).wait_send()
 
+            @pl.when(b == 3)
+            def _():
+                lead_copy(lead, 1, c, 2, 1).wait_send()
+
         @pl.when(odd == 0)
         def _():
             pass_fac(1, b + 1).wait_send()
@@ -302,9 +319,7 @@
     def _():
         for c in range(CHUNKS):
             lead_copy(a_ref, 0, c, 2, 1).wait_send()
-            lead_copy(a_ref, 1, c, 1, 1).wait_send()
-            if nb > 2:
-                lead_copy(a_ref, 1, c, 0, 2).wait_send()
+            lead_copy(a_ref, 1, c, int(nb > 2) ^ 1, 2 if nb > 2 else 1).wait_send()
         pass_fac(1, 1).wait_send()
         if nb > 2:
             pass_fac(0, 2).wait_send()

time: 74.5 us -> 68.6 us (0.921)
  Pallas kernels: 68.2 us -> 62.3 us
    pallas_call x1, Pallas kernels: 68.2 us -> 62.3 us  [on_device(): pl.pallas_call(functools.partial(tile_kernel, nb, npar), out_shape=(jax.S...]
where the time goes in v3:
time: 68.6 us; the launch traced here: 67.3 us
  Pallas kernels  62.3 us (91%)
  local copies, waits for them, and re-layouts  4.43 us (6%)
    pallas_call x1, Pallas kernels, on_device(): pl.pallas_call(functools.partial(tile_kernel, nb, npar), out_shape=(jax.S...  62.3 us
    unnamed x5, local copies, waits for them, and re-layouts  3.18 us

profile of v3, /device:TPU:27, one launch (start us, length us, event | category | flops | bytes accessed | tf_op | source)
XLA Modules:
  0.0 67.3 jit_solution(13946751014150590644)
XLA Ops:
  0.6 0.7 %broadcast_in_dim.2.e_ref = f32[8,256]{1,0:T(8,128)S(1)} broadcast(f32[256]{0:T(256)} %param.3), dimensions={1} | broadcast | bytes 9216 | tf_op jit(solution)/shard_map/broadcast_in_dim | solution.py:361
  1.3 0.0 copy-start
  1.3 1.2 %copy-done = f32[256,1024]{1,0:T(8,128)S(1)} copy-done((f32[256,1024]{1,0:T(8,128)S(1)}, f32[256,1024]{1,0:T(8,128)}, u32[]{:S(2)}) %copy-start) | copy-done | bytes 1048600
  2.5 62.3 %all_tiles.1 = (f32[256,256]{1,0:T(8,128)S(1)}, f32[8,256]{1,0:T(8,128)S(1)}, f32[64,256]{1,0:T(8,128)S(1)}, f32[64,256]{1,0:T(8,128)S(1)}) custom-call(f32[256,1024]{1,0:T(8,128)S(1)} %copy-done, f32[8,256]{1,0:T(8,128)S(1)} %broadcast_in_dim.2.e_ref), custom_call_target="tpu_custom_call" | custom-call | tf_op jit(solution)/shard_map/all_tiles/pallas_call | solution.py:363
  64.8 0.6 slice.3
  65.4 0.7 %copy.9 = f32[256,256]{1,0:T(8,128)} copy(f32[256,256]{1,0:T(8,128)S(1)} %get-tuple-element.16) | data formatting | bytes 524288
  66.1 0.6 copy.10
  66.7 0.6 copy.11
Async XLA Ops:
  1.3 1.2 %copy-start = (f32[256,1024]{1,0:T(8,128)S(1)}, f32[256,1024]{1,0:T(8,128)}, u32[]{:S(2)}) copy-start(f32[256,1024]{1,0:T(8,128)} %a_ref.1) | copy-start | bytes 3145732
